TPU v7x, 32 devices: a whole 2x2x4 slice. The times are simulated.
32 devices in a mesh: groups: 2 (over y), rows: 8 (over z, x), heads: 2 (over core).
Axes of the slice: x: 2, y: 2, z: 4, core: 2. Of those that a mesh axis runs over, the one named last changes fastest.
Arguments:
- residual_in: bfloat16 [128, 8192], P(('groups', 'rows'), 'heads'), parts along dimension 0, may hold values from -6 to 6
- query: bfloat16 [128, 8192], P(('groups', 'rows'), 'heads'), parts along dimension 0, may hold values from -120 to 120
- key_cache: bfloat16 [128, 4, 32, 128], P(('groups', 'rows'), 'heads'), parts along dimension 0, may hold values from -4 to 4
- value_cache: bfloat16 [128, 4, 32, 128], P(('groups', 'rows'), 'heads'), parts along dimension 0, may hold values from -5 to 5
- key_new: bfloat16 [128, 4, 128], P(('groups', 'rows'), 'heads'), parts along dimension 0, may hold values from -4 to 4
- value_new: bfloat16 [128, 4, 128], P(('groups', 'rows'), 'heads'), parts along dimension 0, may hold values from -5 to 5
- lengths: int32 [128], P(('groups', 'rows')), parts along dimension 0, may hold values from 2 to 32, as said below
- norm_gain: bfloat16 [8192], replicated, may hold values from 0.3984375 to 1.59375
- hot_gate: bfloat16 [128, 8192], P('heads'), may hold values from -0.0625 to 0.0625
- hot_up: bfloat16 [128, 8192], P('heads'), may hold values from -0.0625 to 0.0625
- hot_down: bfloat16 [128, 8192], P('heads'), may hold values from -0.5 to 0.5
- cold_gate: bfloat16 [512, 8192], P(('rows', 'heads')), may hold values from -0.0625 to 0.0625
- cold_up: bfloat16 [512, 8192], P(('rows', 'heads')), may hold values from -0.0625 to 0.0625
- cold_down: bfloat16 [512, 8192], P(('rows', 'heads')), may hold values from -0.5 to 0.5
- active: int32 [128, 4], P(('groups', 'rows')), parts along dimension 0, may hold values from 0 to 1, as said below
Outputs:
- residual_out: bfloat16 [128, 8192], P(('groups', 'rows'), 'heads'), parts along dimension 0
There are 2 independent parts, one for each index of `groups`. A program takes and returns all parts, laid end to end along the dimension named above; an argument that names none is the same for every part. Nothing has to cross between parts.
Inputs may be any that keep to these rules, and one draw needn't show every extreme that they name: `lengths`: every request has at least two filled slots, and some request has all 32. `active`: 0 or 1; among the 8 requests of one index of rows at most 2 are active on any one cold block, and exactly 2 on some.
All inputs are finite; a program needn't handle non-finite values.
Results may differ from a plain program's by a relative error of at most 0.0085.
Values may be sent and summed in bfloat16 or wider, within the bound.
A program may use at most 64 MiB of HBM per device.

v0:
```python
import functools

import jax
import jax.numpy as jnp
from jax import lax
from jax.experimental import pallas as pl
from jax.experimental.pallas import tpu as pltpu
from jax.sharding import PartitionSpec as P

HD = 128
GROUP = 16
CAP = 2
REQ = 8
LANES = 512
F32 = jnp.float32
BF16 = jnp.bfloat16
MESH = pl.DeviceIdType.MESH


def iota(shape, axis):
    return lax.broadcasted_iota(jnp.int32, shape, axis)


def div(v, k):
    return lax.shift_right_logical(v, k.bit_length() - 1) if k & (k - 1) == 0 else lax.div(v, k)


def rem(v, k):
    return v & (k - 1) if k & (k - 1) == 0 else lax.rem(v, k)


def onehot(hit):
    return jnp.where(hit, 1.0, 0.0).astype(BF16)


def dot(a, b):
    return jnp.dot(a, b, preferred_element_type=F32)


def dot_t(a, b):
    return lax.dot_general(a, b, (((1,), (1,)), ((), ())), preferred_element_type=F32)


def loop(count, body):
    if count <= 8:
        for step in range(count):
            body(step)
    else:
        lax.fori_loop(0, count, lambda step, carry: (body(step), carry)[1], 0)


def kernel(n, nb, ctx, nhot, ncold, width, *refs):
    (
        q_hbm, res_hbm, kn_hbm, vn_hbm, gain_hbm, len_hbm, act_hbm,
        kc_hbm, vc_hbm, hg_hbm, hu_hbm, hd_hbm, cg_hbm, cu_hbm, cd_hbm,
        out_ref,
        q_ref, res_ref, kn_ref, vn_ref, gain_ref, len_ref, act_ref,
        sel_v, back_v, gather_v, scatter_v,
        kc_v, vc_v, hgu_v, hd_v, cgu_v, cd_v,
        xh, dsp, inc, rout, ret, hot_send, hot_recv, cold_acc,
        load_sem, swap_send, swap_recv, x_sem, hot_sem,
        dsp_sem, inc_sem, rout_sem, ret_sem,
    ) = refs
    half = width // 2
    chunks = half // LANES
    per = n // nb
    row = lax.axis_index("rows")
    h = lax.axis_index("heads")
    other = 1 - h
    t = lax.rem(row, 2)
    idx = lax.div(row, 2)
    partner = {"heads": other}

    loads = [
        (kc_hbm, kc_v),
        (vc_hbm, vc_v),
        (cg_hbm, cgu_v.at[pl.ds(pl.multiple_of(h * ncold, ncold), ncold)]),
        (cu_hbm, cgu_v.at[pl.ds(pl.multiple_of((2 + h) * ncold, ncold), ncold)]),
        (hg_hbm, hgu_v.at[pl.ds(0, nhot)]),
        (hu_hbm, hgu_v.at[pl.ds(nhot, nhot)]),
        (cd_hbm, cd_v.at[pl.ds(pl.multiple_of(h * ncold, ncold), ncold)]),
        (hd_hbm, hd_v),
        (q_hbm, q_ref),
        (kn_hbm, kn_ref),
        (vn_hbm, vn_ref),
        (res_hbm, res_ref),
        (gain_hbm, gain_ref),
        (len_hbm, len_ref),
        (act_hbm, act_ref),
    ]
    loads = [
        pltpu.make_async_copy(src, dst, load_sem.at[i]) for i, (src, dst) in enumerate(loads)
    ]
    for i in (13, 14, 8, 0, 9, 1, 10, 11, 12, 2, 3, 4, 5, 6, 7):
        loads[i].start()

    barrier = pltpu.get_barrier_semaphore()

    def greet(step):
        peer = lax.rem(row + step, n)
        for side in range(2):
            @pl.when(jnp.logical_or(peer != row, h != side))
            def _():
                pl.semaphore_signal(
                    barrier, inc=1, device_id={"rows": peer, "heads": side}, device_id_type=MESH
                )

    loop(n, greet)

    stack = chunks * REQ
    pay = CAP * chunks
    loads[13].wait()
    loads[14].wait()

    def prepare(i):
        targets = []
        for b in range(4):
            count = jnp.int32(0)
            places = [jnp.int32(-1)] * CAP
            for r in range(REQ):
                on = act_ref[i * 4 + b, r]
                for s in range(CAP):
                    places[s] = jnp.where(
                        jnp.logical_and(on == 1, count == s), jnp.int32(r), places[s]
                    )
                count = count + on
            targets += places
        line = iota((4 * pay, 1), 0)
        target = jnp.full((4 * pay, 1), -1, jnp.int32)
        for k, p in enumerate(targets):
            target = jnp.where(div(line, chunks) == k, p, target)
        target = jnp.where(target < 0, -1, rem(line, chunks) * REQ + target)
        sel_v[i] = onehot(iota((4 * pay, stack), 1) == target)
        column = iota((1, 4 * per * pay), 1)
        slot = div(column, pay * per) * CAP + rem(div(column, chunks), CAP)
        target = jnp.full(column.shape, -1, jnp.int32)
        for k, p in enumerate(targets):
            target = jnp.where(slot == k, p, target)
        target = jnp.where(target < 0, -1, rem(column, chunks) * REQ + target)
        back_v[i] = onehot(iota((stack, 4 * per * pay), 0) == target)

    loop(nb // 4, prepare)

    big = 4 * 2 * pay

    def packed(v):
        hf, c = div(v, chunks * 8), rem(div(v, 8), chunks)
        i, s = rem(div(v, 2), 4), rem(v, 2)
        return ((i * 2 + hf) * CAP + s) * chunks + c

    gather_v[...] = onehot(packed(iota((big, 1), 0)) == iota((big, big), 1))
    scatter_v[...] = onehot(packed(iota((1, big), 1)) == iota((big, big), 0))

    scale = 1.0 / HD**0.5
    span = REQ * ctx
    rows_q = GROUP * REQ
    col = iota((1, span), 1)
    whose = jnp.full((1, span), -1, jnp.int32)
    for r in range(REQ):
        here = jnp.logical_and(col >= r * ctx, col < r * ctx + len_ref[r])
        whose = jnp.where(here, r, whose)
    mask = rem(iota((rows_q, span), 0), REQ) == whose

    pl.semaphore_wait(barrier, 2 * n - 1)
    swaps = [
        (cg_hbm, cgu_v.at[pl.ds(pl.multiple_of(h * ncold, ncold), ncold)]),
        (cu_hbm, cgu_v.at[pl.ds(pl.multiple_of((2 + h) * ncold, ncold), ncold)]),
        (cd_hbm, cd_v.at[pl.ds(pl.multiple_of(h * ncold, ncold), ncold)]),
    ]
    swaps = [
        pltpu.make_async_remote_copy(
            src, dst, swap_send.at[i], swap_recv.at[i], device_id=partner, device_id_type=MESH
        )
        for i, (src, dst) in enumerate(swaps)
    ]
    for copy in swaps:
        copy.start()
    for i in (8, 0, 9, 1, 10, 11):
        loads[i].wait()

    q = q_ref[...].astype(F32)
    kv_local = kc_v.shape[1]
    tiles = []

    def attend(g):
        qs = jnp.concatenate(
            [q[:, (g * GROUP + j) * HD:(g * GROUP + j + 1) * HD] for j in range(GROUP)], axis=0
        )
        keys = kc_v[:, g].reshape(span, HD)
        s = dot_t(qs.astype(BF16), keys) * scale
        key_own = jnp.concatenate([kn_ref[:, g, :].astype(F32)] * GROUP, axis=0)
        own = jnp.sum(qs * key_own, axis=-1, keepdims=True) * scale
        s = jnp.where(mask, s, -1e30)
        top = jnp.maximum(jnp.max(s, axis=-1, keepdims=True), own)
        e = jnp.where(mask, jnp.exp(s - top), 0.0)
        e_own = jnp.exp(own - top)
        inv = 1.0 / (jnp.sum(e, axis=-1, keepdims=True) + e_own)
        w = (e * inv).astype(BF16)
        w_own = (e_own * inv).astype(BF16).astype(F32)
        value_own = jnp.concatenate([vn_ref[:, g, :].astype(F32)] * GROUP, axis=0)
        o = dot(w, vc_v[:, g].reshape(span, HD)) + w_own * value_own
        for j in range(GROUP):
            tiles.append(o[j * REQ:(j + 1) * REQ])

    for g in range(kv_local):
        attend(g)

    per_chunk = LANES // HD
    residual = res_ref[...].astype(F32)
    x = jnp.concatenate(
        [
            residual[:, c * LANES:(c + 1) * LANES]
            + jnp.concatenate(tiles[c * per_chunk:(c + 1) * per_chunk], axis=1)
            for c in range(chunks)
        ],
        axis=0,
    ).astype(BF16)
    xh[h] = x

    def select(i):
        dsp[pl.ds(i * 4, 4)] = dot(sel_v[i], x).astype(BF16).reshape(4, pay, LANES)

    loop(nb // 4, select)

    def dispatch(step):
        dst = lax.rem(row + step, n)
        return pltpu.make_async_remote_copy(
            dsp.at[lax.div(dst, per)], inc.at[idx, h], dsp_sem.at[step], inc_sem.at[idx, h],
            device_id={"rows": dst, "heads": t}, device_id_type=MESH,
        )

    dispatch_own = pltpu.make_async_copy(
        dsp.at[lax.div(row, per)], inc.at[idx, h], inc_sem.at[idx, h]
    )
    loop(n - 1, lambda step: dispatch(step + 1).start())

    @pl.when(t == h)
    def _():
        dispatch_own.start()

    @pl.when(t != h)
    def _():
        dispatch(0).start()

    send_x = pltpu.make_async_remote_copy(
        xh.at[h], xh.at[h], x_sem.at[0], x_sem.at[1], device_id=partner, device_id_type=MESH
    )
    send_x.start()

    def hidden(blocks, weights, count):
        total = blocks[0] * blocks[0]
        for block in blocks[1:]:
            total = total + block * block
        rs = lax.rsqrt(jnp.sum(total, axis=-1, keepdims=True) / width + 1e-05)
        normed = jnp.concatenate(
            [
                (
                    block * rs * gain_ref[c * LANES:(c + 1) * LANES].astype(F32)[None, :]
                ).astype(BF16)
                for c, block in enumerate(blocks)
            ],
            axis=1,
        )
        both = dot_t(normed, weights)
        gate, up = both[:, :count], both[:, count:]
        return (gate / (1.0 + jnp.exp(-gate)) * up).astype(BF16)

    loads[4].wait()
    loads[5].wait()
    loads[12].wait()
    send_x.wait()
    whole = [xh[side].astype(F32) for side in range(2)]
    hot_hidden = hidden(
        [whole[c // chunks][(c % chunks) * REQ:(c % chunks + 1) * REQ] for c in range(2 * chunks)],
        hgu_v[...],
        nhot,
    )

    loads[2].wait()
    loads[3].wait()
    loads[6].wait()
    for copy in swaps:
        copy.wait()

    def back(i, hf):
        return pltpu.make_async_remote_copy(
            rout.at[i, hf], ret.at[row], rout_sem.at[i, hf], ret_sem.at[row],
            device_id={"rows": 2 * i + h, "heads": hf}, device_id_type=MESH,
        )

    def mine(i, hf):
        return jnp.logical_and(2 * i + h == row, hf == h)

    def own(i):
        for k in range(4):
            for hf in range(2):
                pltpu.make_async_remote_copy(
                    inc.at[i * 4 + k, hf], inc.at[i * 4 + k, hf],
                    dsp_sem.at[0], inc_sem.at[i * 4 + k, hf],
                    device_id=partner, device_id_type=MESH,
                ).wait_recv()
        y = dot(gather_v[...], inc[pl.ds(i * 4, 4)].reshape(big, LANES))
        hid = hidden([y[c * 8:(c + 1) * 8] for c in range(2 * chunks)], cgu_v[...], 2 * ncold)
        o = dot(hid, cd_v[...])
        o = jnp.concatenate(
            [o[:, c * LANES:(c + 1) * LANES] for c in range(2 * chunks)], axis=0
        ).astype(BF16)
        rout[pl.ds(i * 4, 4)] = dot(scatter_v[...], o).astype(BF16).reshape(4, 2, pay, LANES)
        for k in range(4):
            for hf in range(2):
                @pl.when(mine(i * 4 + k, hf))
                def _():
                    pltpu.make_async_copy(
                        rout.at[i * 4 + k, hf], ret.at[row], ret_sem.at[row]
                    ).start()

                @pl.when(jnp.logical_not(mine(i * 4 + k, hf)))
                def _():
                    back(i * 4 + k, hf).start()

    loop(n // 8, own)

    loads[7].wait()

    def hot_down(side):
        part = dot(hot_hidden, hd_v[:, pl.ds(pl.multiple_of(side * half, half), half)])
        return jnp.concatenate(
            [part[:, c * LANES:(c + 1) * LANES] for c in range(chunks)], axis=0
        )

    hot_send[...] = hot_down(other)
    send_hot = pltpu.make_async_remote_copy(
        hot_send, hot_recv, hot_sem.at[0], hot_sem.at[1], device_id=partner, device_id_type=MESH
    )
    send_hot.start()
    result = hot_down(h) + x.astype(F32)

    cold_acc[...] = result

    def collect(i):
        for k in range(4 * per):
            o = i * 4 * per + k
            pltpu.make_async_remote_copy(
                ret.at[o], ret.at[o], dsp_sem.at[0], ret_sem.at[o],
                device_id=partner, device_id_type=MESH,
            ).wait_recv()
        cold_acc[...] += dot(
            back_v[i], ret[pl.ds(i * 4 * per, 4 * per)].reshape(4 * per * pay, LANES)
        )

    loop(nb // 4, collect)
    send_hot.wait()
    result = cold_acc[...] + hot_recv[...]
    for c in range(chunks):
        out_ref[:, c * LANES:(c + 1) * LANES] = result[c * REQ:(c + 1) * REQ].astype(out_ref.dtype)

    loop(n - 1, lambda step: dispatch(step + 1).wait_send())

    @pl.when(t != h)
    def _():
        dispatch(0).wait_send()

    def drain(i):
        for hf in range(2):
            @pl.when(jnp.logical_not(mine(i, hf)))
            def _():
                back(i, hf).wait_send()

    loop(n // 2, drain)


def local(n, residual_in, query, key_cache, value_cache, key_new, value_new, lengths, norm_gain,
          hot_gate, hot_up, hot_down, cold_gate, cold_up, cold_down, active):
    width = hot_gate.shape[1]
    half = width // 2
    chunks = half // LANES
    nb = active.shape[1]
    nhot, ncold = hot_gate.shape[0], cold_gate.shape[0]
    ctx = key_cache.shape[2]
    vmem = pl.BlockSpec(memory_space=pltpu.VMEM)
    hbm = pl.BlockSpec(memory_space=pltpu.HBM)
    pay = CAP * chunks
    dma = pltpu.SemaphoreType.DMA
    return pl.pallas_call(
        functools.partial(kernel, n, nb, ctx, nhot, ncold, width),
        out_shape=jax.ShapeDtypeStruct(residual_in.shape, residual_in.dtype),
        in_specs=[hbm] * 15,
        out_specs=vmem,
        scratch_shapes=[
            pltpu.VMEM(query.shape, BF16),
            pltpu.VMEM(residual_in.shape, BF16),
            pltpu.VMEM(key_new.shape, BF16),
            pltpu.VMEM(value_new.shape, BF16),
            pltpu.VMEM(norm_gain.shape, BF16),
            pltpu.SMEM(lengths.shape, jnp.int32),
            pltpu.SMEM(active.shape[::-1], jnp.int32),
            pltpu.VMEM((nb // 4, 4 * pay, chunks * REQ), BF16),
            pltpu.VMEM((nb // 4, chunks * REQ, 4 * (n // nb) * pay), BF16),
            pltpu.VMEM((8 * pay, 8 * pay), BF16),
            pltpu.VMEM((8 * pay, 8 * pay), BF16),
            pltpu.VMEM(key_cache.shape, BF16),
            pltpu.VMEM(value_cache.shape, BF16),
            pltpu.VMEM((2 * nhot, width), BF16),
            pltpu.VMEM((nhot, width), BF16),
            pltpu.VMEM((4 * ncold, width), BF16),
            pltpu.VMEM((2 * ncold, width), BF16),
            pltpu.VMEM((2, chunks * REQ, LANES), BF16),
            pltpu.VMEM((nb, pay, LANES), BF16),
            pltpu.VMEM((n // 2, 2, pay, LANES), BF16),
            pltpu.VMEM((n // 2, 2, pay, LANES), BF16),
            pltpu.VMEM((n, pay, LANES), BF16),
            pltpu.VMEM((chunks * REQ, LANES), F32),
            pltpu.VMEM((chunks * REQ, LANES), F32),
            pltpu.VMEM((chunks * REQ, LANES), F32),
            dma((15,)), dma((3,)), dma((3,)), dma((2,)), dma((2,)),
            dma((n,)), dma((n // 2, 2)), dma((n // 2, 2)), dma((n,)),
        ],
        compiler_params=pltpu.CompilerParams(
            collective_id=0, has_side_effects=True, vmem_limit_bytes=64 * 1024 * 1024
        ),
        name="decode_step",
    )(
        query, residual_in, key_new, value_new, norm_gain, lengths, active.T,
        key_cache, value_cache, hot_gate, hot_up, hot_down, cold_gate, cold_up, cold_down,
    )


def solution(mesh):
    return jax.shard_map(
        functools.partial(local, mesh.shape["rows"]),
        mesh=mesh,
        in_specs=(
            P(("groups", "rows"), "heads"),
            P(("groups", "rows"), "heads"),
            P(("groups", "rows"), "heads", None, None),
            P(("groups", "rows"), "heads", None, None),
            P(("groups", "rows"), "heads", None),
            P(("groups", "rows"), "heads", None),
            P(("groups", "rows")),
            P(),
            P("heads", None),
            P("heads", None),
            P("heads", None),
            P(("rows", "heads"), None),
            P(("rows", "heads"), None),
            P(("rows", "heads"), None),
            P(("groups", "rows"), None),
        ),
        out_specs=P(("groups", "rows"), "heads"),
        check_vma=False,
    )
```

profile of v0, /device:TPU:0, one launch (start us, length us, event | category | flops | bytes accessed | tf_op | source)
XLA Modules:
  0.0 21.3 jit_solution(6482556398590207942)
XLA Ops:
  0.0 19.8 %decode_step.1 = bf16[8,4096]{1,0:T(8,128)(2,1)} custom-call(bf16[8,4096]{1,0:T(8,128)(2,1)} %refs_0_.1, bf16[8,4096]{1,0:T(8,128)(2,1)} %refs_1_.1, bf16[8,2,128]{2,1,0:T(2,128)(2,1)} %refs_2_.1, bf16[8,2,128]{2,1,0:T(2,128)(2,1)} %refs_3_.1, bf16[8192]{0:T(1024)(128)(2,1)} %refs_4_.1, s32[8]{0:T(128)} %refs_5_.1, s32[4,8]{1,0:T(4,128)} %bitcast.1, ...), custom_call_target="tpu_custom_call" | custom-call | tf_op jit(solution)/shard_map/decode_step/pallas_call | solution.py:384
  19.8 1.5 %copy.17 = bf16[8,4096]{1,0:T(8,128)(2,1)} copy(bf16[8,4096]{1,0:T(8,128)(2,1)} %decode_step.1) | data formatting | bytes 131072
where the time goes:
time: 21.4 us; the launch traced here: 21.3 us
  Pallas kernels  19.8 us (93%)
  local copies, waits for them, and re-layouts  1.47 us (7%)
    pallas_call x1, Pallas kernels, local(): pl.pallas_call(functools.partial(kernel, n, nb, ctx, nhot, ncold, width),...  19.8 us
    unnamed x1, local copies, waits for them, and re-layouts  1.47 us

commit v1 on v0

--- a/solution.py
+++ b/solution.py
@@ -91,7 +91,7 @@
     loads = [
         pltpu.make_async_copy(src, dst, load_sem.at[i]) for i, (src, dst) in enumerate(loads)
     ]
-    for i in (13, 14, 8, 0, 9, 1, 10, 11, 12, 2, 3, 4, 5, 6, 7):
+    for i in (14, 13, 8, 0, 9, 1, 10, 11, 12):
         loads[i].start()
 
     barrier = pltpu.get_barrier_semaphore()
@@ -161,6 +161,8 @@
         whose = jnp.where(here, r, whose)
     mask = rem(iota((rows_q, span), 0), REQ) == whose
 
+    for i in (2, 3, 6, 4, 5, 7):
+        loads[i].start()
     pl.semaphore_wait(barrier, 2 * n - 1)
     swaps = [
         (cg_hbm, cgu_v.at[pl.ds(pl.multiple_of(h * ncold, ncold), ncold)]),
@@ -195,10 +197,8 @@
         e = jnp.where(mask, jnp.exp(s - top), 0.0)
         e_own = jnp.exp(own - top)
         inv = 1.0 / (jnp.sum(e, axis=-1, keepdims=True) + e_own)
-        w = (e * inv).astype(BF16)
-        w_own = (e_own * inv).astype(BF16).astype(F32)
         value_own = jnp.concatenate([vn_ref[:, g, :].astype(F32)] * GROUP, axis=0)
-        o = dot(w, vc_v[:, g].reshape(span, HD)) + w_own * value_own
+        o = (dot(e.astype(BF16), vc_v[:, g].reshape(span, HD)) + e_own * value_own) * inv
         for j in range(GROUP):
             tiles.append(o[j * REQ:(j + 1) * REQ])
 
@@ -255,13 +255,13 @@
         normed = jnp.concatenate(
             [
                 (
-                    block * rs * gain_ref[c * LANES:(c + 1) * LANES].astype(F32)[None, :]
+                    block * gain_ref[c * LANES:(c + 1) * LANES].astype(F32)[None, :]
                 ).astype(BF16)
                 for c, block in enumerate(blocks)
             ],
             axis=1,
         )
-        both = dot_t(normed, weights)
+        both = dot_t(normed, weights) * rs
         gate, up = both[:, :count], both[:, count:]
         return (gate / (1.0 + jnp.exp(-gate)) * up).astype(BF16)
 
@@ -307,16 +307,15 @@
         ).astype(BF16)
         rout[pl.ds(i * 4, 4)] = dot(scatter_v[...], o).astype(BF16).reshape(4, 2, pay, LANES)
         for k in range(4):
+            far = i * 4 + jnp.where(idx < n // 4, 3 - k, k)
             for hf in range(2):
-                @pl.when(mine(i * 4 + k, hf))
+                @pl.when(mine(far, hf))
                 def _():
-                    pltpu.make_async_copy(
-                        rout.at[i * 4 + k, hf], ret.at[row], ret_sem.at[row]
-                    ).start()
-
-                @pl.when(jnp.logical_not(mine(i * 4 + k, hf)))
+                    pltpu.make_async_copy(rout.at[far, hf], ret.at[row], ret_sem.at[row]).start()
+
+                @pl.when(jnp.logical_not(mine(far, hf)))
                 def _():
-                    back(i * 4 + k, hf).start()
+                    back(far, hf).start()
 
     loop(n // 8, own)
 
@@ -383,7 +382,7 @@
     dma = pltpu.SemaphoreType.DMA
     return pl.pallas_call(
         functools.partial(kernel, n, nb, ctx, nhot, ncold, width),
-        out_shape=jax.ShapeDtypeStruct(residual_in.shape, residual_in.dtype),
+        out_shape=pltpu.VMEM(residual_in.shape, residual_in.dtype),
         in_specs=[hbm] * 15,
         out_specs=vmem,
         scratch_shapes=[
@@ -416,13 +415,16 @@
             dma((n,)), dma((n // 2, 2)), dma((n // 2, 2)), dma((n,)),
         ],
         compiler_params=pltpu.CompilerParams(
-            collective_id=0, has_side_effects=True, vmem_limit_bytes=64 * 1024 * 1024
+            collective_id=0, has_side_effects=True, vmem_limit_bytes=48 * 1024 * 1024
         ),
         name="decode_step",
-    )(
-        query, residual_in, key_new, value_new, norm_gain, lengths, active.T,
-        key_cache, value_cache, hot_gate, hot_up, hot_down, cold_gate, cold_up, cold_down,
-    )
+    )(*[
+        pltpu.with_memory_space_constraint(array, pltpu.HBM)
+        for array in (
+            query, residual_in, key_new, value_new, norm_gain, lengths, active.T,
+            key_cache, value_cache, hot_gate, hot_up, hot_down, cold_gate, cold_up, cold_down,
+        )
+    ])
 
 
 def solution(mesh):

time: 21.4 us -> 19.6 us (0.916)
  Pallas kernels: 19.8 us -> 18.8 us
  local copies, waits for them, and re-layouts: 1.47 us -> 0.63 us
    pallas_call x1, Pallas kernels: 19.8 us -> 18.8 us  [local(): pl.pallas_call(functools.partial(kernel, n, nb, ctx, nhot, ncold, width),...]
    unnamed x1, local copies, waits for them, and re-layouts: 1.47 us -> 0.63 us
where the time goes in v1:
time: 19.6 us; the launch traced here: 19.4 us
  Pallas kernels  18.8 us (96%)
  local copies, waits for them, and re-layouts  0.63 us (3%)
    pallas_call x1, Pallas kernels, local(): pl.pallas_call(functools.partial(kernel, n, nb, ctx, nhot, ncold, width),...  18.8 us
    unnamed x1, local copies, waits for them, and re-layouts  0.63 us

profile of v1, /device:TPU:0, one launch (start us, length us, event | category | flops | bytes accessed | tf_op | source)
XLA Modules:
  0.0 19.4 jit_solution(8328311720092933431)
XLA Ops:
  0.0 18.8 %decode_step.1 = bf16[8,4096]{1,0:T(8,128)(2,1)S(1)} custom-call(bf16[8,4096]{1,0:T(8,128)(2,1)} %refs_0_.1, bf16[8,4096]{1,0:T(8,128)(2,1)} %refs_1_.1, bf16[8,2,128]{2,1,0:T(2,128)(2,1)} %refs_2_.1, bf16[8,2,128]{2,1,0:T(2,128)(2,1)} %refs_3_.1, bf16[8192]{0:T(1024)(128)(2,1)} %refs_4_.1, s32[8]{0:T(128)} %refs_5_.1, s32[4,8]{1,0:T(4,128)} %bitcast.1, ...), custom_call_target="tpu_custom_call" | custom-call | tf_op jit(solution)/shard_map/decode_step/pallas_call | solution.py:383
  18.8 0.6 %copy.17 = bf16[8,4096]{1,0:T(8,128)(2,1)} copy(bf16[8,4096]{1,0:T(8,128)(2,1)S(1)} %decode_step.1) | data formatting | bytes 131072

commit v2 on v1

--- a/solution.py
+++ b/solution.py
@@ -55,7 +55,7 @@
         kc_hbm, vc_hbm, hg_hbm, hu_hbm, hd_hbm, cg_hbm, cu_hbm, cd_hbm,
         out_ref,
         q_ref, res_ref, kn_ref, vn_ref, gain_ref, len_ref, act_ref,
-        sel_v, back_v, gather_v, scatter_v,
+        sel_v, back_v, gather_v, scatter_v, hid_v,
         kc_v, vc_v, hgu_v, hd_v, cgu_v, cd_v,
         xh, dsp, inc, rout, ret, hot_send, hot_recv, cold_acc,
         load_sem, swap_send, swap_recv, x_sem, hot_sem,
@@ -97,15 +97,14 @@
     barrier = pltpu.get_barrier_semaphore()
 
     def greet(step):
-        peer = lax.rem(row + step, n)
+        peer = lax.rem(row + step + 1, n)
         for side in range(2):
-            @pl.when(jnp.logical_or(peer != row, h != side))
-            def _():
-                pl.semaphore_signal(
-                    barrier, inc=1, device_id={"rows": peer, "heads": side}, device_id_type=MESH
-                )
-
-    loop(n, greet)
+            pl.semaphore_signal(
+                barrier, inc=1, device_id={"rows": peer, "heads": side}, device_id_type=MESH
+            )
+
+    pl.semaphore_signal(barrier, inc=1, device_id=partner, device_id_type=MESH)
+    loop(n - 1, greet)
 
     stack = chunks * REQ
     pay = CAP * chunks
@@ -141,42 +140,27 @@
 
     loop(nb // 4, prepare)
 
-    big = 4 * 2 * pay
+    big = 4 * pay
 
     def packed(v):
-        hf, c = div(v, chunks * 8), rem(div(v, 8), chunks)
-        i, s = rem(div(v, 2), 4), rem(v, 2)
-        return ((i * 2 + hf) * CAP + s) * chunks + c
+        return rem(v, 8) * chunks + div(v, 8)
 
     gather_v[...] = onehot(packed(iota((big, 1), 0)) == iota((big, big), 1))
     scatter_v[...] = onehot(packed(iota((1, big), 1)) == iota((big, big), 0))
+    for i in (2, 3, 6, 4, 5, 7):
+        loads[i].start()
 
     scale = 1.0 / HD**0.5
     span = REQ * ctx
     rows_q = GROUP * REQ
-    col = iota((1, span), 1)
-    whose = jnp.full((1, span), -1, jnp.int32)
+    col = iota((1, span + HD), 1)
+    whose = jnp.where(jnp.logical_and(col >= span, col < span + REQ), col - span, -1)
     for r in range(REQ):
         here = jnp.logical_and(col >= r * ctx, col < r * ctx + len_ref[r])
         whose = jnp.where(here, r, whose)
-    mask = rem(iota((rows_q, span), 0), REQ) == whose
-
-    for i in (2, 3, 6, 4, 5, 7):
-        loads[i].start()
-    pl.semaphore_wait(barrier, 2 * n - 1)
-    swaps = [
-        (cg_hbm, cgu_v.at[pl.ds(pl.multiple_of(h * ncold, ncold), ncold)]),
-        (cu_hbm, cgu_v.at[pl.ds(pl.multiple_of((2 + h) * ncold, ncold), ncold)]),
-        (cd_hbm, cd_v.at[pl.ds(pl.multiple_of(h * ncold, ncold), ncold)]),
-    ]
-    swaps = [
-        pltpu.make_async_remote_copy(
-            src, dst, swap_send.at[i], swap_recv.at[i], device_id=partner, device_id_type=MESH
-        )
-        for i, (src, dst) in enumerate(swaps)
-    ]
-    for copy in swaps:
-        copy.start()
+    mask = rem(iota((rows_q, span + HD), 0), REQ) == whose
+    blank = jnp.zeros((HD - REQ, HD), F32)
+    ones = jnp.ones((span + HD, HD), BF16)
     for i in (8, 0, 9, 1, 10, 11):
         loads[i].wait()
 
@@ -188,17 +172,14 @@
         qs = jnp.concatenate(
             [q[:, (g * GROUP + j) * HD:(g * GROUP + j + 1) * HD] for j in range(GROUP)], axis=0
         )
-        keys = kc_v[:, g].reshape(span, HD)
-        s = dot_t(qs.astype(BF16), keys) * scale
-        key_own = jnp.concatenate([kn_ref[:, g, :].astype(F32)] * GROUP, axis=0)
-        own = jnp.sum(qs * key_own, axis=-1, keepdims=True) * scale
-        s = jnp.where(mask, s, -1e30)
-        top = jnp.maximum(jnp.max(s, axis=-1, keepdims=True), own)
-        e = jnp.where(mask, jnp.exp(s - top), 0.0)
-        e_own = jnp.exp(own - top)
-        inv = 1.0 / (jnp.sum(e, axis=-1, keepdims=True) + e_own)
-        value_own = jnp.concatenate([vn_ref[:, g, :].astype(F32)] * GROUP, axis=0)
-        o = (dot(e.astype(BF16), vc_v[:, g].reshape(span, HD)) + e_own * value_own) * inv
+        key_own = jnp.concatenate([kn_ref[:, g, :].astype(F32), blank], axis=0).astype(BF16)
+        keys = jnp.concatenate([kc_v[:, g].reshape(span, HD), key_own], axis=0)
+        s = jnp.where(mask, dot_t(qs.astype(BF16), keys) * scale, -1e30)
+        e = jnp.exp(s - jnp.max(s, axis=-1, keepdims=True))
+        value_own = jnp.concatenate([vn_ref[:, g, :].astype(F32), blank], axis=0).astype(BF16)
+        values = jnp.concatenate([vc_v[:, g].reshape(span, HD), value_own], axis=0)
+        o = dot(e.astype(BF16), jnp.concatenate([values, ones], axis=1))
+        o = o[:, :HD] / o[:, HD:]
         for j in range(GROUP):
             tiles.append(o[j * REQ:(j + 1) * REQ])
 
@@ -222,21 +203,22 @@
 
     loop(nb // 4, select)
 
+    pl.semaphore_wait(barrier, 2 * n - 1)
+
+    side = n // 2
+
     def dispatch(step):
         dst = lax.rem(row + step, n)
         return pltpu.make_async_remote_copy(
-            dsp.at[lax.div(dst, per)], inc.at[idx, h], dsp_sem.at[step], inc_sem.at[idx, h],
+            dsp.at[lax.div(dst, per)], inc.at[h * side + idx], dsp_sem, inc_sem,
             device_id={"rows": dst, "heads": t}, device_id_type=MESH,
         )
 
-    dispatch_own = pltpu.make_async_copy(
-        dsp.at[lax.div(row, per)], inc.at[idx, h], inc_sem.at[idx, h]
-    )
     loop(n - 1, lambda step: dispatch(step + 1).start())
 
     @pl.when(t == h)
     def _():
-        dispatch_own.start()
+        pltpu.make_async_copy(dsp.at[lax.div(row, per)], inc.at[h * side + idx], inc_sem).start()
 
     @pl.when(t != h)
     def _():
@@ -246,6 +228,19 @@
         xh.at[h], xh.at[h], x_sem.at[0], x_sem.at[1], device_id=partner, device_id_type=MESH
     )
     send_x.start()
+    swaps = [
+        (cg_hbm, cgu_v.at[pl.ds(pl.multiple_of(h * ncold, ncold), ncold)]),
+        (cu_hbm, cgu_v.at[pl.ds(pl.multiple_of((2 + h) * ncold, ncold), ncold)]),
+        (cd_hbm, cd_v.at[pl.ds(pl.multiple_of(h * ncold, ncold), ncold)]),
+    ]
+    swaps = [
+        pltpu.make_async_remote_copy(
+            src, dst, swap_send.at[i], swap_recv.at[i], device_id=partner, device_id_type=MESH
+        )
+        for i, (src, dst) in enumerate(swaps)
+    ]
+    for copy in swaps:
+        copy.start()
 
     def hidden(blocks, weights, count):
         total = blocks[0] * blocks[0]
@@ -282,42 +277,70 @@
     for copy in swaps:
         copy.wait()
 
+    def arrive(buffer, sem):
+        pltpu.make_async_remote_copy(
+            buffer, buffer, dsp_sem, sem, device_id=partner, device_id_type=MESH
+        ).wait_recv()
+
+    def drain(buffer, sem):
+        def leave(part):
+            pltpu.make_async_remote_copy(
+                part, part, sem, inc_sem, device_id=partner, device_id_type=MESH
+            ).wait_send()
+
+        leave(buffer.at[pl.ds(0, n - 1)])
+
+        @pl.when(t != h)
+        def _():
+            leave(buffer.at[n - 1])
+
+    arrive(inc, inc_sem)
+
+    def own(i):
+        halves = [
+            dot(gather_v[...], inc[pl.ds(hf * side + i * 4, 4)].reshape(big, LANES))
+            for hf in range(2)
+        ]
+        hid_v[i] = hidden(
+            [halves[c // chunks][(c % chunks) * 8:(c % chunks + 1) * 8] for c in range(2 * chunks)],
+            cgu_v[...],
+            2 * ncold,
+        )
+
+    loop(n // 8, own)
+
     def back(i, hf):
         return pltpu.make_async_remote_copy(
-            rout.at[i, hf], ret.at[row], rout_sem.at[i, hf], ret_sem.at[row],
+            rout.at[hf * side + i], ret.at[row], rout_sem, ret_sem,
             device_id={"rows": 2 * i + h, "heads": hf}, device_id_type=MESH,
         )
 
-    def mine(i, hf):
-        return jnp.logical_and(2 * i + h == row, hf == h)
-
-    def own(i):
-        for k in range(4):
-            for hf in range(2):
-                pltpu.make_async_remote_copy(
-                    inc.at[i * 4 + k, hf], inc.at[i * 4 + k, hf],
-                    dsp_sem.at[0], inc_sem.at[i * 4 + k, hf],
-                    device_id=partner, device_id_type=MESH,
-                ).wait_recv()
-        y = dot(gather_v[...], inc[pl.ds(i * 4, 4)].reshape(big, LANES))
-        hid = hidden([y[c * 8:(c + 1) * 8] for c in range(2 * chunks)], cgu_v[...], 2 * ncold)
-        o = dot(hid, cd_v[...])
-        o = jnp.concatenate(
-            [o[:, c * LANES:(c + 1) * LANES] for c in range(2 * chunks)], axis=0
-        ).astype(BF16)
-        rout[pl.ds(i * 4, 4)] = dot(scatter_v[...], o).astype(BF16).reshape(4, 2, pay, LANES)
-        for k in range(4):
-            far = i * 4 + jnp.where(idx < n // 4, 3 - k, k)
-            for hf in range(2):
-                @pl.when(mine(far, hf))
-                def _():
-                    pltpu.make_async_copy(rout.at[far, hf], ret.at[row], ret_sem.at[row]).start()
-
-                @pl.when(jnp.logical_not(mine(far, hf)))
-                def _():
-                    back(far, hf).start()
-
-    loop(n // 8, own)
+    for hf in range(2):
+        def down(i):
+            o = dot(hid_v[i], cd_v[:, hf * half:(hf + 1) * half])
+            o = jnp.concatenate(
+                [o[:, c * LANES:(c + 1) * LANES] for c in range(chunks)], axis=0
+            ).astype(BF16)
+            rout[pl.ds(hf * side + i * 4, 4)] = (
+                dot(scatter_v[...], o).astype(BF16).reshape(4, pay, LANES)
+            )
+
+        loop(n // 8, down)
+
+        def give(step):
+            offset = jnp.where(idx < side // 2, side - 1 - step, step + 1)
+            back(lax.rem(idx + offset, side), hf).start()
+
+        loop(side - 1, give)
+        here = jnp.logical_and(t == h, h == hf)
+
+        @pl.when(here)
+        def _():
+            pltpu.make_async_copy(rout.at[hf * side + idx], ret.at[row], ret_sem).start()
+
+        @pl.when(jnp.logical_not(here))
+        def _():
+            back(idx, hf).start()
 
     loads[7].wait()
 
@@ -334,15 +357,13 @@
     send_hot.start()
     result = hot_down(h) + x.astype(F32)
 
+    drain(inc, dsp_sem)
+    drain(rout, rout_sem)
+
     cold_acc[...] = result
+    arrive(ret, ret_sem)
 
     def collect(i):
-        for k in range(4 * per):
-            o = i * 4 * per + k
-            pltpu.make_async_remote_copy(
-                ret.at[o], ret.at[o], dsp_sem.at[0], ret_sem.at[o],
-                device_id=partner, device_id_type=MESH,
-            ).wait_recv()
         cold_acc[...] += dot(
             back_v[i], ret[pl.ds(i * 4 * per, 4 * per)].reshape(4 * per * pay, LANES)
         )
@@ -352,20 +373,6 @@
     result = cold_acc[...] + hot_recv[...]
     for c in range(chunks):
         out_ref[:, c * LANES:(c + 1) * LANES] = result[c * REQ:(c + 1) * REQ].astype(out_ref.dtype)
-
-    loop(n - 1, lambda step: dispatch(step + 1).wait_send())
-
-    @pl.when(t != h)
-    def _():
-        dispatch(0).wait_send()
-
-    def drain(i):
-        for hf in range(2):
-            @pl.when(jnp.logical_not(mine(i, hf)))
-            def _():
-                back(i, hf).wait_send()
-
-    loop(n // 2, drain)
 
 
 def local(n, residual_in, query, key_cache, value_cache, key_new, value_new, lengths, norm_gain,
@@ -395,8 +402,9 @@
             pltpu.SMEM(active.shape[::-1], jnp.int32),
             pltpu.VMEM((nb // 4, 4 * pay, chunks * REQ), BF16),
             pltpu.VMEM((nb // 4, chunks * REQ, 4 * (n // nb) * pay), BF16),
-            pltpu.VMEM((8 * pay, 8 * pay), BF16),
-            pltpu.VMEM((8 * pay, 8 * pay), BF16),
+            pltpu.VMEM((4 * pay, 4 * pay), BF16),
+            pltpu.VMEM((4 * pay, 4 * pay), BF16),
+            pltpu.VMEM((n // 8, 8, 2 * ncold), BF16),
             pltpu.VMEM(key_cache.shape, BF16),
             pltpu.VMEM(value_cache.shape, BF16),
             pltpu.VMEM((2 * nhot, width), BF16),
@@ -405,14 +413,14 @@
             pltpu.VMEM((2 * ncold, width), BF16),
             pltpu.VMEM((2, chunks * REQ, LANES), BF16),
             pltpu.VMEM((nb, pay, LANES), BF16),
-            pltpu.VMEM((n // 2, 2, pay, LANES), BF16),
-            pltpu.VMEM((n // 2, 2, pay, LANES), BF16),
+            pltpu.VMEM((n, pay, LANES), BF16),
+            pltpu.VMEM((n, pay, LANES), BF16),
             pltpu.VMEM((n, pay, LANES), BF16),
             pltpu.VMEM((chunks * REQ, LANES), F32),
             pltpu.VMEM((chunks * REQ, LANES), F32),
             pltpu.VMEM((chunks * REQ, LANES), F32),
             dma((15,)), dma((3,)), dma((3,)), dma((2,)), dma((2,)),
-            dma((n,)), dma((n // 2, 2)), dma((n // 2, 2)), dma((n,)),
+            dma(()), dma(()), dma(()), dma(()),
         ],
         compiler_params=pltpu.CompilerParams(
             collective_id=0, has_side_effects=True, vmem_limit_bytes=48 * 1024 * 1024

time: 19.6 us -> 18.5 us (0.944)
  Pallas kernels: 18.8 us -> 17.7 us
    pallas_call x1, Pallas kernels: 18.8 us -> 17.7 us  [local(): pl.pallas_call(functools.partial(kernel, n, nb, ctx, nhot, ncold, width),...]
where the time goes in v2:
time: 18.5 us; the launch traced here: 18.3 us
  Pallas kernels  17.7 us (96%)
  local copies, waits for them, and re-layouts  0.63 us (3%)
    pallas_call x1, Pallas kernels, local(): pl.pallas_call(functools.partial(kernel, n, nb, ctx, nhot, ncold, width),...  17.7 us
    unnamed x1, local copies, waits for them, and re-layouts  0.63 us

profile of v2, /device:TPU:0, one launch (start us, length us, event | category | flops | bytes accessed | tf_op | source)
XLA Modules:
  0.0 18.3 jit_solution(5978630981315429687)
XLA Ops:
  0.0 17.7 %decode_step.1 = bf16[8,4096]{1,0:T(8,128)(2,1)S(1)} custom-call(bf16[8,4096]{1,0:T(8,128)(2,1)} %refs_0_.1, bf16[8,4096]{1,0:T(8,128)(2,1)} %refs_1_.1, bf16[8,2,128]{2,1,0:T(2,128)(2,1)} %refs_2_.1, bf16[8,2,128]{2,1,0:T(2,128)(2,1)} %refs_3_.1, bf16[8192]{0:T(1024)(128)(2,1)} %refs_4_.1, s32[8]{0:T(128)} %refs_5_.1, s32[4,8]{1,0:T(4,128)} %bitcast.1, ...), custom_call_target="tpu_custom_call" | custom-call | tf_op jit(solution)/shard_map/decode_step/pallas_call | solution.py:390
  17.7 0.6 %copy.17 = bf16[8,4096]{1,0:T(8,128)(2,1)} copy(bf16[8,4096]{1,0:T(8,128)(2,1)S(1)} %decode_step.1) | data formatting | bytes 131072

commit v3 on v2

--- a/solution.py
+++ b/solution.py
@@ -164,6 +164,22 @@
     for i in (8, 0, 9, 1, 10, 11):
         loads[i].wait()
 
+    pl.semaphore_wait(barrier, 2 * n - 1)
+
+    swaps = [
+        (cg_hbm, cgu_v.at[pl.ds(pl.multiple_of(h * ncold, ncold), ncold)]),
+        (cu_hbm, cgu_v.at[pl.ds(pl.multiple_of((2 + h) * ncold, ncold), ncold)]),
+        (cd_hbm, cd_v.at[pl.ds(pl.multiple_of(h * ncold, ncold), ncold)]),
+    ]
+    swaps = [
+        pltpu.make_async_remote_copy(
+            src, dst, swap_send.at[i], swap_recv.at[i], device_id=partner, device_id_type=MESH
+        )
+        for i, (src, dst) in enumerate(swaps)
+    ]
+    for copy in swaps:
+        copy.start()
+
     q = q_ref[...].astype(F32)
     kv_local = kc_v.shape[1]
     tiles = []
@@ -203,8 +219,6 @@
 
     loop(nb // 4, select)
 
-    pl.semaphore_wait(barrier, 2 * n - 1)
-
     side = n // 2
 
     def dispatch(step):
@@ -228,20 +242,6 @@
         xh.at[h], xh.at[h], x_sem.at[0], x_sem.at[1], device_id=partner, device_id_type=MESH
     )
     send_x.start()
-    swaps = [
-        (cg_hbm, cgu_v.at[pl.ds(pl.multiple_of(h * ncold, ncold), ncold)]),
-        (cu_hbm, cgu_v.at[pl.ds(pl.multiple_of((2 + h) * ncold, ncold), ncold)]),
-        (cd_hbm, cd_v.at[pl.ds(pl.multiple_of(h * ncold, ncold), ncold)]),
-    ]
-    swaps = [
-        pltpu.make_async_remote_copy(
-            src, dst, swap_send.at[i], swap_recv.at[i], device_id=partner, device_id_type=MESH
-        )
-        for i, (src, dst) in enumerate(swaps)
-    ]
-    for copy in swaps:
-        copy.start()
-
     def hidden(blocks, weights, count):
         total = blocks[0] * blocks[0]
         for block in blocks[1:]:

time: 18.5 us -> 19.1 us (1.032)
  Pallas kernels: 17.7 us -> 18.3 us
    pallas_call x1, Pallas kernels: 17.7 us -> 18.3 us  [local(): pl.pallas_call(functools.partial(kernel, n, nb, ctx, nhot, ncold, width),...]
where the time goes in v3:
time: 19.1 us; the launch traced here: 19 us
  Pallas kernels  18.3 us (96%)
  local copies, waits for them, and re-layouts  0.63 us (3%)
    pallas_call x1, Pallas kernels, local(): pl.pallas_call(functools.partial(kernel, n, nb, ctx, nhot, ncold, width),...  18.3 us
    unnamed x1, local copies, waits for them, and re-layouts  0.63 us

profile of v3, /device:TPU:0, one launch (start us, length us, event | category | flops | bytes accessed | tf_op | source)
XLA Modules:
  0.0 19.0 jit_solution(9180154149634891042)
XLA Ops:
  0.0 18.3 %decode_step.1 = bf16[8,4096]{1,0:T(8,128)(2,1)S(1)} custom-call(bf16[8,4096]{1,0:T(8,128)(2,1)} %refs_0_.1, bf16[8,4096]{1,0:T(8,128)(2,1)} %refs_1_.1, bf16[8,2,128]{2,1,0:T(2,128)(2,1)} %refs_2_.1, bf16[8,2,128]{2,1,0:T(2,128)(2,1)} %refs_3_.1, bf16[8192]{0:T(1024)(128)(2,1)} %refs_4_.1, s32[8]{0:T(128)} %refs_5_.1, s32[4,8]{1,0:T(4,128)} %bitcast.1, ...), custom_call_target="tpu_custom_call" | custom-call | tf_op jit(solution)/shard_map/decode_step/pallas_call | solution.py:390
  18.3 0.6 %copy.17 = bf16[8,4096]{1,0:T(8,128)(2,1)} copy(bf16[8,4096]{1,0:T(8,128)(2,1)S(1)} %decode_step.1) | data formatting | bytes 131072

commit v4 on v2

--- a/solution.py
+++ b/solution.py
@@ -55,7 +55,7 @@
         kc_hbm, vc_hbm, hg_hbm, hu_hbm, hd_hbm, cg_hbm, cu_hbm, cd_hbm,
         out_ref,
         q_ref, res_ref, kn_ref, vn_ref, gain_ref, len_ref, act_ref,
-        sel_v, back_v, gather_v, scatter_v, hid_v,
+        sel_v, back_v, turn_v, hid_v,
         kc_v, vc_v, hgu_v, hd_v, cgu_v, cd_v,
         xh, dsp, inc, rout, ret, hot_send, hot_recv, cold_acc,
         load_sem, swap_send, swap_recv, x_sem, hot_sem,
@@ -70,6 +70,24 @@
     t = lax.rem(row, 2)
     idx = lax.div(row, 2)
     partner = {"heads": other}
+
+    barrier = pltpu.get_barrier_semaphore()
+
+    def greet(peer, core):
+        pl.semaphore_signal(
+            barrier, inc=1, device_id={"rows": peer, "heads": core}, device_id_type=MESH
+        )
+
+    loop(n - 1, lambda step: greet(lax.rem(row + step + 1, n), t))
+    pl.semaphore_signal(barrier, inc=1, device_id=partner, device_id_type=MESH)
+
+    @pl.when(t == h)
+    def _():
+        loop(n // 2 - 1, lambda step: greet(lax.rem(row + 2 * step + 2, n), 1 - t))
+
+    @pl.when(t != h)
+    def _():
+        loop(n // 2, lambda step: greet(lax.rem(row + 2 * step + 1, n), 1 - t))
 
     loads = [
         (kc_hbm, kc_v),
@@ -94,24 +112,12 @@
     for i in (14, 13, 8, 0, 9, 1, 10, 11, 12):
         loads[i].start()
 
-    barrier = pltpu.get_barrier_semaphore()
-
-    def greet(step):
-        peer = lax.rem(row + step + 1, n)
-        for side in range(2):
-            pl.semaphore_signal(
-                barrier, inc=1, device_id={"rows": peer, "heads": side}, device_id_type=MESH
-            )
-
-    pl.semaphore_signal(barrier, inc=1, device_id=partner, device_id_type=MESH)
-    loop(n - 1, greet)
-
     stack = chunks * REQ
     pay = CAP * chunks
     loads[13].wait()
     loads[14].wait()
 
-    def prepare(i):
+    def slots(i):
         targets = []
         for b in range(4):
             count = jnp.int32(0)
@@ -124,29 +130,16 @@
                     )
                 count = count + on
             targets += places
+        return targets
+
+    def prepare(i):
         line = iota((4 * pay, 1), 0)
         target = jnp.full((4 * pay, 1), -1, jnp.int32)
-        for k, p in enumerate(targets):
+        for k, p in enumerate(slots(i)):
             target = jnp.where(div(line, chunks) == k, p, target)
         target = jnp.where(target < 0, -1, rem(line, chunks) * REQ + target)
         sel_v[i] = onehot(iota((4 * pay, stack), 1) == target)
-        column = iota((1, 4 * per * pay), 1)
-        slot = div(column, pay * per) * CAP + rem(div(column, chunks), CAP)
-        target = jnp.full(column.shape, -1, jnp.int32)
-        for k, p in enumerate(targets):
-            target = jnp.where(slot == k, p, target)
-        target = jnp.where(target < 0, -1, rem(column, chunks) * REQ + target)
-        back_v[i] = onehot(iota((stack, 4 * per * pay), 0) == target)
-
     loop(nb // 4, prepare)
-
-    big = 4 * pay
-
-    def packed(v):
-        return rem(v, 8) * chunks + div(v, 8)
-
-    gather_v[...] = onehot(packed(iota((big, 1), 0)) == iota((big, big), 1))
-    scatter_v[...] = onehot(packed(iota((1, big), 1)) == iota((big, big), 0))
     for i in (2, 3, 6, 4, 5, 7):
         loads[i].start()
 
@@ -203,7 +196,7 @@
 
     loop(nb // 4, select)
 
-    pl.semaphore_wait(barrier, 2 * n - 1)
+    pl.semaphore_wait(barrier, n + n // 2 - jnp.where(t == h, 1, 0))
 
     side = n // 2
 
@@ -241,6 +234,17 @@
     ]
     for copy in swaps:
         copy.start()
+
+    def prepare_back(i):
+        column = iota((1, 4 * per * pay), 1)
+        slot = div(column, pay * per) * CAP + rem(div(column, chunks), CAP)
+        target = jnp.full(column.shape, -1, jnp.int32)
+        for k, p in enumerate(slots(i)):
+            target = jnp.where(slot == k, p, target)
+        target = jnp.where(target < 0, -1, rem(column, chunks) * REQ + target)
+        back_v[i] = onehot(iota((stack, 4 * per * pay), 0) == target)
+
+    loop(nb // 4, prepare_back)
 
     def hidden(blocks, weights, count):
         total = blocks[0] * blocks[0]
@@ -294,15 +298,25 @@
         def _():
             leave(buffer.at[n - 1])
 
+    big = 4 * pay
     arrive(inc, inc_sem)
 
     def own(i):
-        halves = [
-            dot(gather_v[...], inc[pl.ds(hf * side + i * 4, 4)].reshape(big, LANES))
-            for hf in range(2)
-        ]
+        for hf in range(2):
+            came = inc[pl.ds(hf * side + i * 4, 4)].reshape(big, LANES).astype(F32)
+            for l in range(per_chunk):
+                turn_v[hf, l] = came[:, l * HD:(l + 1) * HD]
         hid_v[i] = hidden(
-            [halves[c // chunks][(c % chunks) * 8:(c % chunks + 1) * 8] for c in range(2 * chunks)],
+            [
+                jnp.concatenate(
+                    [
+                        turn_v[c // chunks, l, pl.ds(c % chunks, 8, stride=chunks)]
+                        for l in range(per_chunk)
+                    ],
+                    axis=1,
+                )
+                for c in range(2 * chunks)
+            ],
             cgu_v[...],
             2 * ncold,
         )
@@ -318,12 +332,13 @@
     for hf in range(2):
         def down(i):
             o = dot(hid_v[i], cd_v[:, hf * half:(hf + 1) * half])
-            o = jnp.concatenate(
-                [o[:, c * LANES:(c + 1) * LANES] for c in range(chunks)], axis=0
-            ).astype(BF16)
-            rout[pl.ds(hf * side + i * 4, 4)] = (
-                dot(scatter_v[...], o).astype(BF16).reshape(4, pay, LANES)
-            )
+            for c in range(chunks):
+                for l in range(per_chunk):
+                    turn_v[hf, l, pl.ds(c, 8, stride=chunks)] = (
+                        o[:, c * LANES + l * HD:c * LANES + (l + 1) * HD]
+                    )
+            turned = jnp.concatenate([turn_v[hf, l] for l in range(per_chunk)], axis=1)
+            rout[pl.ds(hf * side + i * 4, 4)] = turned.astype(BF16).reshape(4, pay, LANES)
 
         loop(n // 8, down)
 
@@ -402,8 +417,7 @@
             pltpu.SMEM(active.shape[::-1], jnp.int32),
             pltpu.VMEM((nb // 4, 4 * pay, chunks * REQ), BF16),
             pltpu.VMEM((nb // 4, chunks * REQ, 4 * (n // nb) * pay), BF16),
-            pltpu.VMEM((4 * pay, 4 * pay), BF16),
-            pltpu.VMEM((4 * pay, 4 * pay), BF16),
+            pltpu.VMEM((2, LANES // HD, 4 * pay, HD), F32),
             pltpu.VMEM((n // 8, 8, 2 * ncold), BF16),
             pltpu.VMEM(key_cache.shape, BF16),
             pltpu.VMEM(value_cache.shape, BF16),

time: 18.5 us -> 18.2 us (0.984)
  Pallas kernels: 17.7 us -> 17.4 us
    pallas_call x1, Pallas kernels: 17.7 us -> 17.4 us  [local(): pl.pallas_call(functools.partial(kernel, n, nb, ctx, nhot, ncold, width),...]
where the time goes in v4:
time: 18.2 us; the launch traced here: 18 us
  Pallas kernels  17.4 us (96%)
  local copies, waits for them, and re-layouts  0.63 us (3%)
    pallas_call x1, Pallas kernels, local(): pl.pallas_call(functools.partial(kernel, n, nb, ctx, nhot, ncold, width),...  17.4 us
    unnamed x1, local copies, waits for them, and re-layouts  0.63 us

profile of v4, /device:TPU:0, one launch (start us, length us, event | category | flops | bytes accessed | tf_op | source)
XLA Modules:
  0.0 18.0 jit_solution(737435888621027401)
XLA Ops:
  0.0 17.4 %decode_step.1 = bf16[8,4096]{1,0:T(8,128)(2,1)S(1)} custom-call(bf16[8,4096]{1,0:T(8,128)(2,1)} %refs_0_.1, bf16[8,4096]{1,0:T(8,128)(2,1)} %refs_1_.1, bf16[8,2,128]{2,1,0:T(2,128)(2,1)} %refs_2_.1, bf16[8,2,128]{2,1,0:T(2,128)(2,1)} %refs_3_.1, bf16[8192]{0:T(1024)(128)(2,1)} %refs_4_.1, s32[8]{0:T(128)} %refs_5_.1, s32[4,8]{1,0:T(4,128)} %bitcast.1, ...), custom_call_target="tpu_custom_call" | custom-call | tf_op jit(solution)/shard_map/decode_step/pallas_call | solution.py:405
  17.4 0.6 %copy.17 = bf16[8,4096]{1,0:T(8,128)(2,1)} copy(bf16[8,4096]{1,0:T(8,128)(2,1)S(1)} %decode_step.1) | data formatting | bytes 131072

commit v5 on v4

--- a/solution.py
+++ b/solution.py
@@ -221,17 +221,22 @@
         xh.at[h], xh.at[h], x_sem.at[0], x_sem.at[1], device_id=partner, device_id_type=MESH
     )
     send_x.start()
-    swaps = [
-        (cg_hbm, cgu_v.at[pl.ds(pl.multiple_of(h * ncold, ncold), ncold)]),
-        (cu_hbm, cgu_v.at[pl.ds(pl.multiple_of((2 + h) * ncold, ncold), ncold)]),
-        (cd_hbm, cd_v.at[pl.ds(pl.multiple_of(h * ncold, ncold), ncold)]),
-    ]
-    swaps = [
-        pltpu.make_async_remote_copy(
-            src, dst, swap_send.at[i], swap_recv.at[i], device_id=partner, device_id_type=MESH
-        )
-        for i, (src, dst) in enumerate(swaps)
-    ]
+    swaps = []
+    for hbm, held, base in ((cg_hbm, cgu_v, h), (cu_hbm, cgu_v, 2 + h), (cd_hbm, cd_v, h)):
+        for line in range(0, ncold, ncold // 2):
+            lines = pl.ds(pl.multiple_of(base * ncold + line, ncold // 2), ncold // 2)
+            for hf in range(2):
+                columns = pl.ds(hf * half, half)
+                swaps.append(
+                    pltpu.make_async_remote_copy(
+                        hbm.at[pl.ds(line, ncold // 2), columns],
+                        held.at[lines, columns],
+                        swap_send.at[len(swaps)],
+                        swap_recv.at[len(swaps)],
+                        device_id=partner,
+                        device_id_type=MESH,
+                    )
+                )
     for copy in swaps:
         copy.start()
 
@@ -433,7 +438,7 @@
             pltpu.VMEM((chunks * REQ, LANES), F32),
             pltpu.VMEM((chunks * REQ, LANES), F32),
             pltpu.VMEM((chunks * REQ, LANES), F32),
-            dma((15,)), dma((3,)), dma((3,)), dma((2,)), dma((2,)),
+            dma((15,)), dma((12,)), dma((12,)), dma((2,)), dma((2,)),
             dma(()), dma(()), dma(()), dma(()),
         ],
         compiler_params=pltpu.CompilerParams(

time: 18.2 us -> 18.3 us (level)
  no operation moved by 1% of the time
where the time goes in v5:
time: 18.3 us; the launch traced here: 18.2 us
  Pallas kernels  17.5 us (96%)
  local copies, waits for them, and re-layouts  0.63 us (3%)
    pallas_call x1, Pallas kernels, local(): pl.pallas_call(functools.partial(kernel, n, nb, ctx, nhot, ncold, width),...  17.5 us
    unnamed x1, local copies, waits for them, and re-layouts  0.63 us

profile of v5, /device:TPU:0, one launch (start us, length us, event | category | flops | bytes accessed | tf_op | source)
XLA Modules:
  0.0 18.2 jit_solution(14477950174734644542)
XLA Ops:
  0.0 17.5 %decode_step.1 = bf16[8,4096]{1,0:T(8,128)(2,1)S(1)} custom-call(bf16[8,4096]{1,0:T(8,128)(2,1)} %refs_0_.1, bf16[8,4096]{1,0:T(8,128)(2,1)} %refs_1_.1, bf16[8,2,128]{2,1,0:T(2,128)(2,1)} %refs_2_.1, bf16[8,2,128]{2,1,0:T(2,128)(2,1)} %refs_3_.1, bf16[8192]{0:T(1024)(128)(2,1)} %refs_4_.1, s32[8]{0:T(128)} %refs_5_.1, s32[4,8]{1,0:T(4,128)} %bitcast.1, ...), custom_call_target="tpu_custom_call" | custom-call | tf_op jit(solution)/shard_map/decode_step/pallas_call | solution.py:410
  17.5 0.6 %copy.17 = bf16[8,4096]{1,0:T(8,128)(2,1)} copy(bf16[8,4096]{1,0:T(8,128)(2,1)S(1)} %decode_step.1) | data formatting | bytes 131072

commit v6 on v4

--- a/solution.py
+++ b/solution.py
@@ -264,17 +264,7 @@
         gate, up = both[:, :count], both[:, count:]
         return (gate / (1.0 + jnp.exp(-gate)) * up).astype(BF16)
 
-    loads[4].wait()
-    loads[5].wait()
     loads[12].wait()
-    send_x.wait()
-    whole = [xh[side].astype(F32) for side in range(2)]
-    hot_hidden = hidden(
-        [whole[c // chunks][(c % chunks) * REQ:(c % chunks + 1) * REQ] for c in range(2 * chunks)],
-        hgu_v[...],
-        nhot,
-    )
-
     loads[2].wait()
     loads[3].wait()
     loads[6].wait()
@@ -356,6 +346,16 @@
         @pl.when(jnp.logical_not(here))
         def _():
             back(idx, hf).start()
+
+    loads[4].wait()
+    loads[5].wait()
+    send_x.wait()
+    whole = [xh[side].astype(F32) for side in range(2)]
+    hot_hidden = hidden(
+        [whole[c // chunks][(c % chunks) * REQ:(c % chunks + 1) * REQ] for c in range(2 * chunks)],
+        hgu_v[...],
+        nhot,
+    )
 
     loads[7].wait()
 

time: 18.2 us -> 18.2 us (level)
  no operation moved by 1% of the time
where the time goes in v6:
time: 18.2 us; the launch traced here: 18.1 us
  Pallas kernels  17.4 us (96%)
  local copies, waits for them, and re-layouts  0.63 us (3%)
    pallas_call x1, Pallas kernels, local(): pl.pallas_call(functools.partial(kernel, n, nb, ctx, nhot, ncold, width),...  17.4 us
    unnamed x1, local copies, waits for them, and re-layouts  0.63 us

profile of v6, /device:TPU:0, one launch (start us, length us, event | category | flops | bytes accessed | tf_op | source)
XLA Modules:
  0.0 18.1 jit_solution(76238212883602958)
XLA Ops:
  0.0 17.4 %decode_step.1 = bf16[8,4096]{1,0:T(8,128)(2,1)S(1)} custom-call(bf16[8,4096]{1,0:T(8,128)(2,1)} %refs_0_.1, bf16[8,4096]{1,0:T(8,128)(2,1)} %refs_1_.1, bf16[8,2,128]{2,1,0:T(2,128)(2,1)} %refs_2_.1, bf16[8,2,128]{2,1,0:T(2,128)(2,1)} %refs_3_.1, bf16[8192]{0:T(1024)(128)(2,1)} %refs_4_.1, s32[8]{0:T(128)} %refs_5_.1, s32[4,8]{1,0:T(4,128)} %bitcast.1, ...), custom_call_target="tpu_custom_call" | custom-call | tf_op jit(solution)/shard_map/decode_step/pallas_call | solution.py:405
  17.4 0.6 %copy.17 = bf16[8,4096]{1,0:T(8,128)(2,1)} copy(bf16[8,4096]{1,0:T(8,128)(2,1)S(1)} %decode_step.1) | data formatting | bytes 131072
